TPU v7x, 32 devices: a whole 2x2x4 slice. The times are simulated.
32 devices in a mesh: groups: 2 (over y), row: 16 (over z, x, core).
Axes of the slice: x: 2, y: 2, z: 4, core: 2. Of those that a mesh axis runs over, the one named last changes fastest.
Arguments:
- p_tiles: bfloat16 [128, 64, 1024], P(('groups', 'row')), parts along dimension 0, may hold values from -0.59765625 to 0.59765625
- p_cols: int32 [128, 16], P(('groups', 'row')), parts along dimension 0, may hold values from 0 to 63, as said below
- p_count: int32 [128], P(('groups', 'row')), parts along dimension 0, may hold values from 8 to 16, as said below
- m_tiles: bfloat16 [128, 64, 1024], P(('groups', 'row')), parts along dimension 0, may hold values from -0.75 to 0.75
- m_cols: int32 [128, 16], P(('groups', 'row')), parts along dimension 0, may hold values from 0 to 63, as said below
- m_count: int32 [128], P(('groups', 'row')), parts along dimension 0, may hold values from 8 to 16, as said below
- g_tiles: bfloat16 [128, 3, 64, 1024], P(('groups', 'row')), parts along dimension 0, may hold values from -0.023925781 to 0.023925781
- basis_atom: int32 [8192], P('groups'), parts along dimension 0, may hold values from 0 to 639, never falling along the last dimension, each value on 1 to 12 neighbouring positions
- atom_slot: int32 [1280], P('groups'), parts along dimension 0, may hold values from 0 to 639, each once
Outputs:
- w_tiles: float32 [128, 64, 1024], P(('groups', 'row')), parts along dimension 0
- forces: float32 [3, 1280], P(None, ('groups', 'row')), parts along dimension 1
There are 2 independent parts, one for each index of `groups`. A program takes and returns all parts, laid end to end along the dimension named above; each array names one. Nothing has to cross between parts.
Inputs may be any that keep to these rules, and one draw needn't show every extreme that they name: `p_cols`: each tile row n lists 16 different tile columns, each within 8 of n counted around the cycle of 64 tile columns. `m_cols`: each tile row n lists 16 different tile columns, each within 8 of n counted around the cycle of 64 tile columns. `p_count`: the live slots of a tile row come first; some tile row has all 16 live in every draw. `m_count`: the live slots of a tile row come first; some tile row has all 16 live in every draw.
All inputs are finite; a program needn't handle non-finite values.
Results may differ from a plain program's by a relative error of at most 0.005.
Values may be sent and summed in bfloat16 or wider, within the bound.
A program may use at most 128 MiB of HBM per device.

v0:
```python
import jax
import jax.numpy as jnp
from jax import lax
from jax.sharding import PartitionSpec as P

BAND = 8


def passed_along(array, axis, by):
    length = lax.axis_size(axis)
    return lax.ppermute(array, axis, [(i, (i + by) % length) for i in range(length)])


def fetch_rows(panel_set, reach):
    below_list = []
    moving = panel_set
    for stride in range(reach):
        moving = passed_along((moving[0], moving[1], moving[2]), "row", 1)
        below_list = [moving] + below_list
    above_list = []
    moving = panel_set
    for stride in range(reach):
        moving = passed_along((moving[0], moving[1], moving[2]), "row", -1)
        above_list = above_list + [moving]
    members = below_list + [panel_set] + above_list
    return tuple((jnp.concatenate([member[place] for member in members], 0) for place in range(3)))


def band_form(tiles, cols, counts, first_row, cycle_rows, lead_pad, band_width):
    tile_rows, tile_size, flat_width = tiles.shape
    slot_count = flat_width // tile_size
    tile_grid = tiles.reshape(tile_rows, tile_size, slot_count, tile_size)
    global_rows = (first_row + jnp.arange(tile_rows, dtype=jnp.int32)) % cycle_rows
    offset_index = (cols - global_rows[:, None] + BAND) % cycle_rows + lead_pad
    is_live = jnp.arange(slot_count, dtype=jnp.int32)[None, :] < counts[:, None]
    selector = (
        offset_index[:, :, None] == jnp.arange(band_width, dtype=jnp.int32)[None, None, :]
    ) & is_live[:, :, None]
    banded = jnp.einsum(
        "kasb,ksf->kafb",
        tile_grid,
        selector.astype(jnp.bfloat16),
        preferred_element_type=jnp.float32,
    )
    return banded.astype(jnp.bfloat16)


def body(p_tiles, p_cols, p_count, m_tiles, m_cols, m_count, g_tiles, basis_atom, atom_slot):
    tile_rows, tile_size, flat_width = p_tiles.shape
    slot_count = flat_width // tile_size
    cycle_rows = tile_rows * lax.axis_size("row")
    first_row = lax.axis_index("row") * tile_rows
    reach_m = -(-BAND // tile_rows)
    reach_p = -(-(2 * BAND) // tile_rows)
    band_span = 2 * BAND + 1
    m_fetched = fetch_rows((m_tiles, m_cols, m_count), reach_m)
    p_fetched = fetch_rows((p_tiles, p_cols, p_count), reach_p)
    m_start = reach_m * tile_rows - BAND
    m_length = tile_rows + 2 * BAND
    m_band = band_form(
        m_fetched[0],
        m_fetched[1],
        m_fetched[2],
        first_row - BAND,
        cycle_rows,
        2 * BAND,
        6 * BAND + 1,
    )
    p_start = reach_p * tile_rows - 2 * BAND
    p_length = tile_rows + 4 * BAND
    p_band = band_form(
        p_fetched[0], p_fetched[1], p_fetched[2], first_row - 2 * BAND, cycle_rows, 0, band_span
    )
    span_index = jnp.arange(band_span, dtype=jnp.int32)
    skew_rows = jnp.arange(tile_rows + 2 * BAND, dtype=jnp.int32)[:, None] + span_index[None, :]
    flipped = 2 * BAND - span_index
    skewed = p_band[skew_rows, :, flipped[None, :], :]
    own_grid = p_tiles.reshape(tile_rows, tile_size, slot_count, tile_size)
    own_live = jnp.arange(slot_count, dtype=jnp.int32)[None, :] < p_count[:, None]
    own_grid = jnp.where(own_live[:, None, :, None], own_grid, jnp.zeros((), own_grid.dtype))

    def one_row(local):
        global_row = first_row + local
        offsets = (p_cols[local] - global_row + BAND) % cycle_rows - BAND
        m_pieces = jax.vmap(
            lambda row_at, start: lax.dynamic_slice(
                m_band, (row_at, 0, start, 0), (1, tile_size, 4 * BAND + 1, tile_size)
            )[0]
        )(local + offsets + BAND, BAND - offsets)
        x_row = jnp.einsum(
            "asb,sboc->aoc", own_grid[local], m_pieces, preferred_element_type=jnp.float32
        ).astype(jnp.bfloat16)
        x_pieces = jax.vmap(lambda start: lax.dynamic_slice_in_dim(x_row, start, band_span, 1))(
            offsets + BAND
        )
        p_pieces = skewed[local + offsets + BAND]
        w_row = jnp.einsum("saub,subc->asc", x_pieces, p_pieces, preferred_element_type=jnp.float32)
        return jnp.where(own_live[local][None, :, None], w_row, 0.0)

    w_grid = lax.map(one_row, jnp.arange(tile_rows, dtype=jnp.int32))
    w_tiles = w_grid.reshape(tile_rows, tile_size, flat_width)
    g_grid = g_tiles.reshape(tile_rows, 3, tile_size, slot_count, tile_size).astype(jnp.float32)
    row_sums = jnp.einsum("kcasb,kasb->kca", g_grid, w_grid)
    col_sums = jnp.einsum("kcasb,kasb->kcsb", g_grid, w_grid)
    first_basis = first_row * tile_size
    row_atoms = lax.dynamic_slice_in_dim(basis_atom, first_basis, tile_rows * tile_size)
    col_basis = (
        p_cols[:, :, None] * tile_size + jnp.arange(tile_size, dtype=jnp.int32)[None, None, :]
    ).reshape(-1)
    col_atoms = basis_atom[col_basis]
    atom_count = atom_slot.shape[0]
    force_terms = jnp.zeros((3, atom_count), jnp.float32)
    force_terms = force_terms.at[:, atom_slot[row_atoms]].add(
        row_sums.transpose(1, 0, 2).reshape(3, -1)
    )
    force_terms = force_terms.at[:, atom_slot[col_atoms]].add(
        -col_sums.transpose(1, 0, 2, 3).reshape(3, -1)
    )
    owned_forces = lax.psum_scatter(force_terms, "row", scatter_dimension=1, tiled=True)
    return (w_tiles, -2.0 * owned_forces)


def solution(mesh):
    return jax.shard_map(
        body,
        mesh=mesh,
        in_specs=(
            P(("groups", "row"), None, None),
            P(("groups", "row"), None),
            P(("groups", "row")),
            P(("groups", "row"), None, None),
            P(("groups", "row"), None),
            P(("groups", "row")),
            P(("groups", "row"), None, None, None),
            P("groups"),
            P("groups"),
        ),
        out_specs=(P(("groups", "row"), None, None), P(None, ("groups", "row"))),
        check_vma=False,
    )
```

profile of v0, /device:TPU:0, one launch (start us, length us, event | category | flops | bytes accessed | tf_op | source)
XLA Modules:
  0.0 506.8 jit_solution(18023061274246565169)
XLA Ops:
  17.8 23.0 %gather_fusion.5 = s32[4096]{0:T(1024)S(1)} fusion(s32[4096]{0:T(1024)S(1)} %copy-done.2, s32[4096]{0:T(1024)S(1)} %broadcast_clamp_fusion.1), kind=kCustom, calls=%fused_computation.5 | custom fusion | bytes 49152 | tf_op jit(solution)/shard_map/gather | solution.py:110
  40.9 16.7 %gather_fusion.6 = s32[4096]{0:T(1024)S(1)} fusion(s32[640]{0:T(1024)S(1)} %copy-done, s32[4096]{0:T(1024)S(1)} %broadcast_clamp_fusion), kind=kCustom, calls=%fused_computation.6 | custom fusion | bytes 49152 | tf_op jit(solution)/shard_map/gather | solution.py:116
  73.1 5.7 %collective-permute-done.28 = s32[4]{0:T(128)S(1)} collective-permute-done((s32[4]{0:T(128)S(1)}, s32[4]{0:T(128)S(1)}, u32[]{:S(2)}, u32[]{:S(2)}) %collective-permute-start.28) | collective-permute-done | bytes 48 | tf_op jit(solution)/shard_map/ppermute | solution.py:11
  80.0 5.6 %collective-permute-done.9 = s32[4]{0:T(128)S(1)} collective-permute-done((s32[4]{0:T(128)S(1)}, s32[4]{0:T(128)S(1)}, u32[]{:S(2)}, u32[]{:S(2)}) %collective-permute-start.9) | collective-permute-done | bytes 48 | tf_op jit(solution)/shard_map/ppermute | solution.py:11
  135.0 5.8 %collective-permute-done.3 = s32[4,16]{0,1:T(8,128)S(1)} collective-permute-done((s32[4,16]{0,1:T(8,128)S(1)}, s32[4,16]{0,1:T(8,128)S(1)}, u32[]{:S(2)}, u32[]{:S(2)}) %collective-permute-start.3) | collective-permute-done | bytes 288 | tf_op jit(solution)/shard_map/ppermute | solution.py:11
  164.6 9.0 %collective-permute-start.19 = (bf16[4,64,1024]{2,1,0:T(8,128)(2,1)}, bf16[4,64,1024]{2,1,0:T(8,128)(2,1)S(1)}, u32[]{:S(2)}, u32[]{:S(2)}) collective-permute-start(bf16[4,64,1024]{2,1,0:T(8,128)(2,1)} %collective-permute-done.18), channel_id=1, source_target_pairs={{0,1},{1,2},{2,3},{3,4},{4,5},{5,6},{6,7},{7,8},{8,9},{9,10},{10,1... | collective-permute-start | bytes 1572872 | tf_op jit(solution)/shard_map/ppermute | solution.py:11
  173.6 10.7 %convert_bitcast_fusion = bf16[20,64,49,64]{3,2,1,0:T(8,128)(2,1)} fusion(bf16[20,64,16,64]{3,2,1,0:T(8,128)(2,1)} %reshape.489, s32[20,16]{1,0:T(8,128)S(1)} %fusion.28, pred[20,16]{1,0:T(8,128)(4,1)S(1)} %iota_compare_fusion.3), kind=kOutput, calls=%fused_computation.35 | convolution fusion | flops 132496000 | bytes 10651200 | tf_op jit(solution)/shard_map/kasb,ksf->kafb/dot_general | solution.py:39
  184.3 15.2 %copy.39 = bf16[20,64,49,64]{3,1,0,2:T(8,128)(2,1)} copy(bf16[20,64,49,64]{3,2,1,0:T(8,128)(2,1)} %convert_bitcast_fusion) | data formatting | bytes 16056320 | tf_op jit(solution)/shard_map/while | solution.py:100
  216.6 13.1 %reshape.487 = bf16[36,64,16,64]{3,2,1,0:T(8,128)(2,1)} reshape(bf16[36,64,1024]{2,1,0:T(8,128)(2,1)} %constant_dynamic-update-slice_fusion) | data formatting | bytes 9437184 | tf_op jit(solution)/shard_map/reshape | solution.py:32
  229.7 6.6 %convert_bitcast_fusion.1 = bf16[36,64,17,64]{3,2,1,0:T(8,128)(2,1)S(1)} fusion(bf16[36,64,16,64]{3,2,1,0:T(8,128)(2,1)} %reshape.487, s32[36,16]{1,0:T(8,128)S(1)} %copy.36, pred[36,16]{1,0:T(8,128)(4,1)S(1)} %iota_compare_fusion.2), kind=kOutput, calls=%fused_computation.36 | convolution fusion | flops 82742400 | bytes 9734976 | tf_op jit(solution)/shard_map/kasb,ksf->kafb/dot_general | solution.py:39
  241.5 9.2 %gather_fusion.3 = bf16[340,64,64]{2,1,0:T(8,128)(2,1)} fusion(bf16[36,64,17,64]{3,1,2,0:T(8,128)(2,1)} %copy.37, s32[340]{0:T(512)S(1)} %reshape.514), kind=kCustom, calls=%fused_computation.3 | custom fusion | bytes 5573280 | tf_op jit(solution)/shard_map/gather | solution.py:77
  250.6 141.6 %while.14 = (s32[]{:T(128)}, f32[4,64,16,64]{1,3,2,0:T(8,128)S(1)}, s32[4]{0:T(128)S(1)}, pred[4,16]{1,0:T(4,128)(4,1)S(1)}, s32[4,16]{1,0:T(4,128)}, /*index=5*...) while((s32[]{:T(128)}, f32[4,64,16,64]{1,3,2,0:T(8,128)S(1)}, ...), condition=%wide.region_1.2_spmd, body=%wide.region_0.1_spmd.sunk | while | flops 419632672 | bytes 27539112 | solution.py:100
  255.1 10.7 %gather_fusion.1 = bf16[16,64,33,64]{3,1,2,0:T(8,128)(2,1)} fusion(bf16[20,64,49,64]{3,1,0,2:T(8,128)(2,1)} %get-tuple-element.349, s32[16]{0:T(128)S(1)} %get-tuple-element.315), kind=kCustom, calls=%fused_computation.1.clone.1 | custom fusion | bytes 8651008 | tf_op jit(solution)/shard_map/while/body/eval_jaxpr/vmap()/gather | solution.py:86
  275.2 5.8 %gather_fusion = bf16[16,17,64,64]{3,2,1,0:T(8,128)(2,1)} fusion(bf16[20,17,64,64]{3,2,1,0:T(8,128)(2,1)} %get-tuple-element.347, s32[1024]{0:T(1024)S(1)} %pad_clamp_fusion.3), kind=kCustom, calls=%fused_computation.clone.1 | custom fusion | bytes 4456512 | tf_op jit(solution)/shard_map/while/body/eval_jaxpr/gather | solution.py:96
  290.6 10.7 %gather_fusion.1 = bf16[16,64,33,64]{3,1,2,0:T(8,128)(2,1)} fusion(bf16[20,64,49,64]{3,1,0,2:T(8,128)(2,1)} %get-tuple-element.349, s32[16]{0:T(128)S(1)} %get-tuple-element.315), kind=kCustom, calls=%fused_computation.1.clone.1 | custom fusion | bytes 8651008 | tf_op jit(solution)/shard_map/while/body/eval_jaxpr/vmap()/gather | solution.py:86
  310.6 5.8 %gather_fusion = bf16[16,17,64,64]{3,2,1,0:T(8,128)(2,1)} fusion(bf16[20,17,64,64]{3,2,1,0:T(8,128)(2,1)} %get-tuple-element.347, s32[1024]{0:T(1024)S(1)} %pad_clamp_fusion.3), kind=kCustom, calls=%fused_computation.clone.1 | custom fusion | bytes 4456512 | tf_op jit(solution)/shard_map/while/body/eval_jaxpr/gather | solution.py:96
  326.0 10.7 %gather_fusion.1 = bf16[16,64,33,64]{3,1,2,0:T(8,128)(2,1)} fusion(bf16[20,64,49,64]{3,1,0,2:T(8,128)(2,1)} %get-tuple-element.349, s32[16]{0:T(128)S(1)} %get-tuple-element.315), kind=kCustom, calls=%fused_computation.1.clone.1 | custom fusion | bytes 8651008 | tf_op jit(solution)/shard_map/while/body/eval_jaxpr/vmap()/gather | solution.py:86
  346.0 5.8 %gather_fusion = bf16[16,17,64,64]{3,2,1,0:T(8,128)(2,1)} fusion(bf16[20,17,64,64]{3,2,1,0:T(8,128)(2,1)} %get-tuple-element.347, s32[1024]{0:T(1024)S(1)} %pad_clamp_fusion.3), kind=kCustom, calls=%fused_computation.clone.1 | custom fusion | bytes 4456512 | tf_op jit(solution)/shard_map/while/body/eval_jaxpr/gather | solution.py:96
  361.4 10.7 %gather_fusion.1 = bf16[16,64,33,64]{3,1,2,0:T(8,128)(2,1)} fusion(bf16[20,64,49,64]{3,1,0,2:T(8,128)(2,1)} %get-tuple-element.349, s32[16]{0:T(128)S(1)} %get-tuple-element.315), kind=kCustom, calls=%fused_computation.1.clone.1 | custom fusion | bytes 8651008 | tf_op jit(solution)/shard_map/while/body/eval_jaxpr/vmap()/gather | solution.py:86
  381.4 5.8 %gather_fusion = bf16[16,17,64,64]{3,2,1,0:T(8,128)(2,1)} fusion(bf16[20,17,64,64]{3,2,1,0:T(8,128)(2,1)} %get-tuple-element.347, s32[1024]{0:T(1024)S(1)} %pad_clamp_fusion.3), kind=kCustom, calls=%fused_computation.clone.1 | custom fusion | bytes 4456512 | tf_op jit(solution)/shard_map/while/body/eval_jaxpr/gather | solution.py:96
  396.7 8.3 %fusion.13 = f32[4,64,1,3,1]{3,2,4,1,0:T(1,128)S(1)} fusion(bf16[4,64,16,64,1]{3,4,2,1,0:T(2,128)(2,1)} %copy.47, bf16[4,3,64,16,64]{4,3,2,1,0:T(8,128)(2,1)} %copy-done.3), kind=kOutput, calls=%fused_computation.37 | convolution fusion | flops 1572864 | bytes 2100224 | tf_op jit(solution)/shard_map/kcasb,kasb->kca/dot_general | solution.py:103
  405.0 8.2 %fusion.37 = f32[4,16,64,1,3]{4,3,2,1,0:T(1,128)} fusion(f32[4,64,16,64,1]{1,4,3,2,0:T(1,128)S(1)} %bitcast.120, bf16[4,3,64,16,64]{2,1,4,3,0:T(4,128)(2,1)} %copy.51), kind=kOutput, calls=%fused_computation.106 | convolution fusion | flops 1572864 | bytes 2670592 | tf_op jit(solution)/shard_map/kcasb,kasb->kcsb/dot_general | solution.py:104
  418.8 26.1 %scatter_fusion = f32[3,640]{0,1:T(8,128)S(1)} fusion(f32[3,640]{0,1:T(8,128)S(1)} %scatter_custom_fusion, s32[4096]{0:T(1024)S(1)} %bitcast.124, f32[4096,3]{1,0:T(8,128)} %bitcast.122), kind=kCustom, calls=%fused_computation.8 | custom fusion | flops 12288 | bytes 163840 | tf_op jit(solution)/shard_map/scatter-add | solution.py:116
  447.2 51.4 %reduce-scatter.4.cloned.1.call-done = f32[3,40]{0,1:T(8,128)} async-done(((f32[3,640]{0,1:T(8,128)}), f32[3,40]{0,1:T(8,128)}) %reduce-scatter.4.cloned.1.call-update) | async-done | bytes 496
  (186 shorter events, 201.8 us)
Async XLA Ops:
  7.2 491.4 %reduce-scatter.4.cloned.1.call-start = ((), (), s32[]{:S(2)}) async-start(), calls=%async_computation.1 | async-start | bytes 348160
  8.0 99.9 %collective-permute-start = (s32[4,16]{0,1:T(8,128)S(1)}, s32[4,16]{0,1:T(8,128)S(1)}, u32[]{:S(2)}, u32[]{:S(2)}) collective-permute-start(s32[4,16]{0,1:T(8,128)S(1)} %copy.33), channel_id=1, source_target_pairs={{0,1},{1,2},{2,3},{3,4},{4,5},{5,6},{6,7},{7,8},{8,9},{9,10},{10,1... | collective-permute-start | bytes 776 | tf_op jit(solution)/shard_map/ppermute | solution.py:11
  8.5 103.9 %collective-permute-start.4 = (s32[4,16]{0,1:T(8,128)S(1)}, s32[4,16]{0,1:T(8,128)S(1)}, u32[]{:S(2)}, u32[]{:S(2)}) collective-permute-start(s32[4,16]{0,1:T(8,128)S(1)} %copy.33), channel_id=1, source_target_pairs={{0,15},{1,0},{2,1},{3,2},{4,3},{5,4},{6,5},{7,6},{8,7},{9,8},{10,9... | collective-permute-start | bytes 776 | tf_op jit(solution)/shard_map/ppermute | solution.py:11
  13.4 121.4 %collective-permute-start.16 = (bf16[4,64,1024]{2,1,0:T(8,128)(2,1)}, bf16[4,64,1024]{2,1,0:T(8,128)(2,1)}, u32[]{:S(2)}, u32[]{:S(2)}) collective-permute-start(bf16[4,64,1024]{2,1,0:T(8,128)(2,1)} %param.11), channel_id=1, source_target_pairs={{0,1},{1,2},{2,3},{3,4},{4,5},{5,6},{6,7},{7,8},{8,9},{9,10},{10,1... | collective-permute-start | bytes 1572872 | tf_op jit(solution)/shard_map/ppermute | solution.py:11
  13.4 53.9 %collective-permute-start.8 = (s32[4]{0:T(128)}, s32[4]{0:T(128)S(1)}, u32[]{:S(2)}, u32[]{:S(2)}) collective-permute-start(s32[4]{0:T(128)} %param.13), channel_id=1, source_target_pairs={{0,1},{1,2},{2,3},{3,4},{4,5},{5,6},{6,7},{7,8},{8,9},{9,10},{10,1... | collective-permute-start | bytes 56 | tf_op jit(solution)/shard_map/ppermute | solution.py:11
  13.4 121.4 %collective-permute-start.32 = (bf16[4,64,1024]{2,1,0:T(8,128)(2,1)}, bf16[4,64,1024]{2,1,0:T(8,128)(2,1)}, u32[]{:S(2)}, u32[]{:S(2)}) collective-permute-start(bf16[4,64,1024]{2,1,0:T(8,128)(2,1)} %param.14), channel_id=1, source_target_pairs={{0,1},{1,2},{2,3},{3,4},{4,5},{5,6},{6,7},{7,8},{8,9},{9,10},{10,1... | collective-permute-start | bytes 1572872 | tf_op jit(solution)/shard_map/ppermute | solution.py:11
  107.9 9.7 %collective-permute-start.24 = (s32[4,16]{1,0:T(4,128)S(1)}, s32[4,16]{1,0:T(4,128)S(1)}, u32[]{:S(2)}, u32[]{:S(2)}) collective-permute-start(s32[4,16]{1,0:T(4,128)S(1)} %copy-done.9), channel_id=1, source_target_pairs={{0,1},{1,2},{2,3},{3,4},{4,5},{5,6},{6,7},{7,8},{8,9},{9,10},{10,1... | collective-permute-start | bytes 776 | tf_op jit(solution)/shard_map/ppermute | solution.py:11
  107.9 14.1 %collective-permute-start.26 = (s32[4,16]{1,0:T(4,128)S(1)}, s32[4,16]{1,0:T(4,128)S(1)}, u32[]{:S(2)}, u32[]{:S(2)}) collective-permute-start(s32[4,16]{1,0:T(4,128)S(1)} %copy-done.9), channel_id=1, source_target_pairs={{0,15},{1,0},{2,1},{3,2},{4,3},{5,4},{6,5},{7,6},{8,7},{9,8},{10,9... | collective-permute-start | bytes 776 | tf_op jit(solution)/shard_map/ppermute | solution.py:11
  112.3 9.7 %collective-permute-start.1 = (s32[4,16]{0,1:T(8,128)S(1)}, s32[4,16]{0,1:T(8,128)S(1)}, u32[]{:S(2)}, u32[]{:S(2)}) collective-permute-start(s32[4,16]{0,1:T(8,128)S(1)} %collective-permute-done), channel_id=1, source_target_pairs={{0,1},{1,2},{2,3},{3,4},{4,5},{5,6},{6,7},{7,8},{8,9},{9,10},{10,1... | collective-permute-start | bytes 776 | tf_op jit(solution)/shard_map/ppermute | solution.py:11
  117.6 9.0 %collective-permute-start.5 = (s32[4,16]{0,1:T(8,128)S(1)}, s32[4,16]{0,1:T(8,128)S(1)}, u32[]{:S(2)}, u32[]{:S(2)}) collective-permute-start(s32[4,16]{0,1:T(8,128)S(1)} %collective-permute-done.4), channel_id=1, source_target_pairs={{0,15},{1,0},{2,1},{3,2},{4,3},{5,4},{6,5},{7,6},{8,7},{9,8},{10,9... | collective-permute-start | bytes 776 | tf_op jit(solution)/shard_map/ppermute | solution.py:11
  122.0 5.8 %collective-permute-start.25 = (s32[4,16]{1,0:T(4,128)S(1)}, s32[4,16]{1,0:T(4,128)S(1)}, u32[]{:S(2)}, u32[]{:S(2)}) collective-permute-start(s32[4,16]{1,0:T(4,128)S(1)} %collective-permute-done.24), channel_id=1, source_target_pairs={{0,1},{1,2},{2,3},{3,4},{4,5},{5,6},{6,7},{7,8},{8,9},{9,10},{10,1... | collective-permute-start | bytes 776 | tf_op jit(solution)/shard_map/ppermute | solution.py:11
  126.5 15.7 %collective-permute-start.34 = (bf16[4,64,1024]{2,1,0:T(8,128)(2,1)}, bf16[4,64,1024]{2,1,0:T(8,128)(2,1)}, u32[]{:S(2)}, u32[]{:S(2)}) collective-permute-start(bf16[4,64,1024]{2,1,0:T(8,128)(2,1)} %param.14), channel_id=1, source_target_pairs={{0,15},{1,0},{2,1},{3,2},{4,3},{5,4},{6,5},{7,6},{8,7},{9,8},{10,9... | collective-permute-start | bytes 1572872 | tf_op jit(solution)/shard_map/ppermute | solution.py:11
  127.8 5.9 %collective-permute-start.2 = (s32[4,16]{0,1:T(8,128)S(1)}, s32[4,16]{0,1:T(8,128)S(1)}, u32[]{:S(2)}, u32[]{:S(2)}) collective-permute-start(s32[4,16]{0,1:T(8,128)S(1)} %collective-permute-done.1), channel_id=1, source_target_pairs={{0,1},{1,2},{2,3},{3,4},{4,5},{5,6},{6,7},{7,8},{8,9},{9,10},{10,1... | collective-permute-start | bytes 776 | tf_op jit(solution)/shard_map/ppermute | solution.py:11
  127.8 7.0 %collective-permute-start.6 = (s32[4,16]{0,1:T(8,128)S(1)}, s32[4,16]{0,1:T(8,128)S(1)}, u32[]{:S(2)}, u32[]{:S(2)}) collective-permute-start(s32[4,16]{0,1:T(8,128)S(1)} %collective-permute-done.5), channel_id=1, source_target_pairs={{0,15},{1,0},{2,1},{3,2},{4,3},{5,4},{6,5},{7,6},{8,7},{9,8},{10,9... | collective-permute-start | bytes 776 | tf_op jit(solution)/shard_map/ppermute | solution.py:11
  133.7 13.3 %collective-permute-start.20 = (bf16[4,64,1024]{2,1,0:T(8,128)(2,1)}, bf16[4,64,1024]{2,1,0:T(8,128)(2,1)S(1)}, u32[]{:S(2)}, u32[]{:S(2)}) collective-permute-start(bf16[4,64,1024]{2,1,0:T(8,128)(2,1)} %param.11), channel_id=1, source_target_pairs={{0,15},{1,0},{2,1},{3,2},{4,3},{5,4},{6,5},{7,6},{8,7},{9,8},{10,9... | collective-permute-start | bytes 1572872 | tf_op jit(solution)/shard_map/ppermute | solution.py:11
  134.8 6.0 %collective-permute-start.3 = (s32[4,16]{0,1:T(8,128)S(1)}, s32[4,16]{0,1:T(8,128)S(1)}, u32[]{:S(2)}, u32[]{:S(2)}) collective-permute-start(s32[4,16]{0,1:T(8,128)S(1)} %collective-permute-done.2), channel_id=1, source_target_pairs={{0,1},{1,2},{2,3},{3,4},{4,5},{5,6},{6,7},{7,8},{8,9},{9,10},{10,1... | collective-permute-start | bytes 776 | tf_op jit(solution)/shard_map/ppermute | solution.py:11
  134.8 13.0 %collective-permute-start.17 = (bf16[4,64,1024]{2,1,0:T(8,128)(2,1)}, bf16[4,64,1024]{2,1,0:T(8,128)(2,1)}, u32[]{:S(2)}, u32[]{:S(2)}) collective-permute-start(bf16[4,64,1024]{2,1,0:T(8,128)(2,1)} %collective-permute-done.16), channel_id=1, source_target_pairs={{0,1},{1,2},{2,3},{3,4},{4,5},{5,6},{6,7},{7,8},{8,9},{9,10},{10,1... | collective-permute-start | bytes 1572872 | tf_op jit(solution)/shard_map/ppermute | solution.py:11
  134.8 17.6 %collective-permute-start.33 = (bf16[4,64,1024]{2,1,0:T(8,128)(2,1)}, bf16[4,64,1024]{2,1,0:T(8,128)(2,1)}, u32[]{:S(2)}, u32[]{:S(2)}) collective-permute-start(bf16[4,64,1024]{2,1,0:T(8,128)(2,1)} %collective-permute-done.32), channel_id=1, source_target_pairs={{0,1},{1,2},{2,3},{3,4},{4,5},{5,6},{6,7},{7,8},{8,9},{9,10},{10,1... | collective-permute-start | bytes 1572872 | tf_op jit(solution)/shard_map/ppermute | solution.py:11
  142.3 14.4 %collective-permute-start.35 = (bf16[4,64,1024]{2,1,0:T(8,128)(2,1)}, bf16[4,64,1024]{2,1,0:T(8,128)(2,1)}, u32[]{:S(2)}, u32[]{:S(2)}) collective-permute-start(bf16[4,64,1024]{2,1,0:T(8,128)(2,1)} %collective-permute-done.34), channel_id=1, source_target_pairs={{0,15},{1,0},{2,1},{3,2},{4,3},{5,4},{6,5},{7,6},{8,7},{9,8},{10,9... | collective-permute-start | bytes 1572872 | tf_op jit(solution)/shard_map/ppermute | solution.py:11
  147.0 15.8 %collective-permute-start.21 = (bf16[4,64,1024]{2,1,0:T(8,128)(2,1)S(1)}, bf16[4,64,1024]{2,1,0:T(8,128)(2,1)}, u32[]{:S(2)}, u32[]{:S(2)}) collective-permute-start(bf16[4,64,1024]{2,1,0:T(8,128)(2,1)S(1)} %collective-permute-done.20), channel_id=1, source_target_pairs={{0,15},{1,0},{2,1},{3,2},{4,3},{5,4},{6,5},{7,6},{8,7},{9,8},{10,9... | collective-permute-start | bytes 1572872 | tf_op jit(solution)/shard_map/ppermute | solution.py:11
  147.8 16.8 %collective-permute-start.18 = (bf16[4,64,1024]{2,1,0:T(8,128)(2,1)}, bf16[4,64,1024]{2,1,0:T(8,128)(2,1)}, u32[]{:S(2)}, u32[]{:S(2)}) collective-permute-start(bf16[4,64,1024]{2,1,0:T(8,128)(2,1)} %collective-permute-done.17), channel_id=1, source_target_pairs={{0,1},{1,2},{2,3},{3,4},{4,5},{5,6},{6,7},{7,8},{8,9},{9,10},{10,1... | collective-permute-start | bytes 1572872 | tf_op jit(solution)/shard_map/ppermute | solution.py:11
  162.7 36.8 %collective-permute-start.22 = (bf16[4,64,1024]{2,1,0:T(8,128)(2,1)}, bf16[4,64,1024]{2,1,0:T(8,128)(2,1)S(1)}, u32[]{:S(2)}, u32[]{:S(2)}) collective-permute-start(bf16[4,64,1024]{2,1,0:T(8,128)(2,1)} %collective-permute-done.21), channel_id=1, source_target_pairs={{0,15},{1,0},{2,1},{3,2},{4,3},{5,4},{6,5},{7,6},{8,7},{9,8},{10,9... | collective-permute-start | bytes 1572872 | tf_op jit(solution)/shard_map/ppermute | solution.py:11
  164.6 40.3 %collective-permute-start.19 = (bf16[4,64,1024]{2,1,0:T(8,128)(2,1)}, bf16[4,64,1024]{2,1,0:T(8,128)(2,1)S(1)}, u32[]{:S(2)}, u32[]{:S(2)}) collective-permute-start(bf16[4,64,1024]{2,1,0:T(8,128)(2,1)} %collective-permute-done.18), channel_id=1, source_target_pairs={{0,1},{1,2},{2,3},{3,4},{4,5},{5,6},{6,7},{7,8},{8,9},{9,10},{10,1... | collective-permute-start | bytes 1572872 | tf_op jit(solution)/shard_map/ppermute | solution.py:11
  199.6 16.2 %collective-permute-start.23 = (bf16[4,64,1024]{2,1,0:T(8,128)(2,1)S(1)}, bf16[4,64,1024]{2,1,0:T(8,128)(2,1)S(1)}, u32[]{:S(2)}, u32[]{:S(2)}) collective-permute-start(bf16[4,64,1024]{2,1,0:T(8,128)(2,1)S(1)} %collective-permute-done.22), channel_id=1, source_target_pairs={{0,15},{1,0},{2,1},{3,2},{4,3},{5,4},{6,5},{7,6},{8,7},{9,8},{10,9... | collective-permute-start | bytes 1572872 | tf_op jit(solution)/shard_map/ppermute | solution.py:11
  (25 other events, 358.7 us)
Sparse Core Ops, SparseCore 0:
  445.8 52.7 reduce-scatter.3
where the time goes:
time: 509 us; the launch traced here: 507 us
  local copies, waits for them, and re-layouts  211 us (41%)
  waiting for transfers between devices  102 us (20%)
  matrix products  74.7 us (15%)
  starting transfers between devices  50.7 us (10%)
  other arithmetic  44.7 us (9%)
  between operations  14.4 us (3%)
  loops' own time  10.3 us (2%)
    unnamed x2, waiting for transfers between devices  51.4 us
    ppermute x36, starting transfers between devices, passed_along(): lax.ppermute(array, axis, [(i, (i + by) % length) for i in range(length)])  50.7 us
    ppermute x36, waiting for transfers between devices, passed_along(): lax.ppermute(array, axis, [(i, (i + by) % length) for i in range(length)])  50.1 us
    gather x4, local copies, waits for them, and re-layouts, one_row(): lax.dynamic_slice(m_band, (row_at, 0, start, 0), (1, tile_size, 4 * BAND...  42.7 us
    scatter-add x1, other arithmetic, body(): force_terms.at[:, atom_slot[col_atoms]]  26.1 us
    gather x4, local copies, waits for them, and re-layouts, one_row(): p_pieces = skewed[local + offsets + BAND]  23.1 us
    gather x1, local copies, waits for them, and re-layouts, body(): col_atoms = basis_atom[col_basis]  23 us
    dot_general x4, matrix products, one_row(): jnp.einsum('asb,sboc->aoc', own_grid[local], m_pieces, preferred_element_...  20.5 us
  transfers between devices with their start and end apart: 37, of which 17 were waited for; matrix products, arithmetic and copies ran while one was open for 21% of the time, Pallas kernels for 0%

commit v1 on v0

v1 whole, which is shorter than its diff:
```python
import functools
import jax
import jax.numpy as jnp
from jax import lax
from jax.experimental import pallas as pl
from jax.experimental.pallas import tpu as pltpu
from jax.sharding import PartitionSpec as P

BAND = 8
L = 128
F32 = jnp.float32
BF = jnp.bfloat16
MESH = pl.DeviceIdType.MESH


def kernel(n, inv_p, inv_m, idx_w, p_ref, m_ref, g_ref, cid_ref, w_ref, f_ref,
           pt, mt, gt, pfull, gfull, mbuf, pbuf, xacc, xb, wacc, wt, onehot,
           ms, mr, ps, pr):
    me = lax.axis_index("row")
    core = lax.rem(me, 2)
    sibling = me + 1 - 2 * core

    def at(shift):
        return lax.rem(me + shift + n, n)

    up1, dn1, up2, dn2 = at(2), at(-2), at(4), at(-4)
    barrier = pltpu.get_barrier_semaphore()
    for peer in (sibling, up1, dn1, up2, dn2):
        pl.semaphore_signal(barrier, inc=1, device_id={"row": peer}, device_id_type=MESH)

    def rows(at_super, count=2):
        return pl.ds(pl.multiple_of(at_super * L, L), count * L)

    def split(src, r, dst):
        for p in range(8):
            v = src[:, p * L:(p + 1) * L]
            dst[2 * p, r * 64:(r + 1) * 64, :] = v[:, :64]
            dst[2 * p + 1, r * 64:(r + 1) * 64, :] = v[:, 64:]
        dst[16, r * 64:(r + 1) * 64, :] = jnp.zeros((64, 64), BF)

    def pick(src, inv, r, u):
        a = src[inv[r, 2 * u], r * 64:(r + 1) * 64, :]
        b = src[inv[r, 2 * u + 1], r * 64:(r + 1) * 64, :]
        return jnp.concatenate([a, b], axis=1)

    for r in range(4):
        split(m_ref.at[r], r, mt)
        sup = r // 2
        for u in range(sup, sup + 9):
            mbuf[pl.ds(pl.multiple_of((4 + 2 * core) * L, L) + r * 64, 64),
                 (u - sup) * L:(u - sup + 1) * L] = pick(mt, inv_m, r, u)
    pl.semaphore_wait(barrier, 5)

    def copy(buf, src_at, dst_at, col, width, sends, recvs, i, peer):
        cols = pl.ds(col, width * L)
        return pltpu.make_async_remote_copy(
            src_ref=buf.at[rows(src_at), cols], dst_ref=buf.at[rows(dst_at), cols],
            send_sem=sends.at[i], recv_sem=recvs.at[i],
            device_id={"row": peer}, device_id_type=MESH)

    own_m = 4 + 2 * core
    m_up = copy(mbuf, own_m, 2 * core, 0, 9, ms, mr, 0, up1)
    m_dn = copy(mbuf, own_m, 8 + 2 * core, 0, 9, ms, mr, 1, dn1)
    m_sib = copy(mbuf, own_m, own_m, 0, 9, ms, mr, 2, sibling)
    f_at = 8 - 6 * core
    m_fwd = copy(mbuf, f_at, f_at, 0, 9, ms, mr, 3, sibling)
    m_up.start()
    m_dn.start()
    m_sib.start()

    own_p = 8 + 2 * core
    for r in range(4):
        split(p_ref.at[r], r, pt)
        sup = r // 2
        for u in range(10):
            if sup <= u < sup + 9:
                v = pick(pt, inv_p, r, u)
                pfull[r * 64:(r + 1) * 64, u * L:(u + 1) * L] = v
                pbuf[pl.ds(pl.multiple_of(own_p * L, L) + r * 64, 64),
                     (u - sup) * L:(u - sup + 1) * L] = v
            else:
                pfull[r * 64:(r + 1) * 64, u * L:(u + 1) * L] = jnp.zeros((64, L), BF)
    p_up = copy(pbuf, own_p, 4 + 2 * core, L, 8, ps, pr, 0, up1)
    p_dn = copy(pbuf, own_p, 12 + 2 * core, 0, 8, ps, pr, 1, dn1)
    p_up2 = copy(pbuf, own_p, 2 * core, 5 * L, 4, ps, pr, 2, up2)
    p_dn2 = copy(pbuf, own_p, 16 + 2 * core, 0, 4, ps, pr, 3, dn2)
    p_sib = copy(pbuf, own_p, own_p, 0, 9, ps, pr, 4, sibling)
    p_fwd_a = copy(pbuf, 4 + 2 * core, 4 + 2 * core, L, 8, ps, pr, 5, sibling)
    p_fwd_b = copy(pbuf, 12 + 2 * core, 12 + 2 * core, 0, 8, ps, pr, 6, sibling)
    far_at = 16 - 14 * core
    p_fwd_c = copy(pbuf, far_at, far_at, pl.multiple_of(core * 5 * L, L), 4, ps, pr, 7, sibling)
    for c in (p_up, p_dn, p_up2, p_dn2, p_sib):
        c.start()

    for c in range(3):
        for r in range(4):
            split(g_ref.at[r, c], r, gt)
            for u in range(10):
                gfull[c, r * 64:(r + 1) * 64, u * L:(u + 1) * L] = pick(gt, inv_p, r, u)
    slots = onehot.shape[1]
    for s in range(slots // L):
        ids = lax.broadcasted_iota(jnp.int32, (10 * L, L), 1) + s * L
        onehot[:, s * L:(s + 1) * L] = jnp.where(cid_ref[...] == ids, 1.0, 0.0).astype(BF)

    xacc[...] = jnp.zeros(xacc.shape, F32)
    wacc[...] = jnp.zeros(wacc.shape, F32)

    def add_x(j):
        xacc[:, j * L:(j + 9) * L] += jnp.dot(
            pfull[:, j * L:(j + 1) * L], mbuf[rows(j + 2 * core, 1), :],
            preferred_element_type=F32)

    def add_w(k):
        q0, q1 = max(0, 8 - k), min(8, 17 - k)
        m0 = k + q0 - 8
        width = q1 - q0 + 1
        wacc[:, m0 * L:(m0 + width) * L] += jnp.dot(
            xb[:, k * L:(k + 1) * L],
            pbuf[rows(k + 2 * core, 1), q0 * L:(q1 + 1) * L],
            preferred_element_type=F32)

    add_x(4)
    add_x(5)
    m_up.wait_recv()
    m_dn.wait_recv()
    m_fwd.start()
    for j in (0, 1, 8, 9):
        add_x(j)
    m_sib.wait_recv()
    m_fwd.wait_recv()
    for j in (2, 3, 6, 7):
        add_x(j)
    xb[...] = xacc[...].astype(BF)
    add_w(8)
    add_w(9)
    p_up.wait_recv()
    p_fwd_a.start()
    p_dn.wait_recv()
    p_fwd_b.start()
    for k in (4, 5, 12, 13):
        add_w(k)
    p_up2.wait_recv()
    p_dn2.wait_recv()
    p_fwd_c.start()
    for k in (0, 1, 16, 17):
        add_w(k)
    p_sib.wait_recv()
    p_fwd_a.wait_recv()
    p_fwd_b.wait_recv()
    for k in (6, 7, 10, 11):
        add_w(k)
    p_fwd_c.wait_recv()
    for k in (2, 3, 14, 15):
        add_w(k)

    lane = lax.broadcasted_iota(jnp.int32, (4 * 64, L), 1)
    by_row = jnp.zeros((4 * 64, L), F32)
    sub = lax.broadcasted_iota(jnp.int32, (8, 10 * L), 0)
    by_col = jnp.zeros((8, 10 * L), F32)
    for c in range(3):
        prod = wacc[...] * gfull[c].astype(F32)
        by_row = jnp.where(lane == c, jnp.sum(prod, axis=1, keepdims=True), by_row)
        by_col = jnp.where(sub == c, jnp.sum(prod, axis=0, keepdims=True), by_col)
    net_rows = jnp.transpose(by_row)[:8]
    net = jnp.concatenate(
        [-by_col[:, :4 * L], net_rows - by_col[:, 4 * L:6 * L], -by_col[:, 6 * L:]], axis=1)
    high = net.astype(BF).astype(F32)
    rest = net - high
    mid = rest.astype(BF).astype(F32)
    low = rest - mid
    parts = jnp.concatenate([high, mid, low, jnp.zeros_like(low)], axis=0).astype(BF)
    summed = jnp.dot(parts, onehot[...], preferred_element_type=F32)
    f_ref[...] = -2.0 * (summed[0:8] + summed[8:16] + summed[16:24])

    for t in range(20):
        wt[t] = wacc[:, t * 64:(t + 1) * 64]
    wt[20] = jnp.zeros((4 * 64, 64), F32)
    for r in range(4):
        for p in range(8):
            a = wt[idx_w[r, 2 * p], r * 64:(r + 1) * 64, :]
            b = wt[idx_w[r, 2 * p + 1], r * 64:(r + 1) * 64, :]
            w_ref[r, :, p * L:(p + 1) * L] = jnp.concatenate([a, b], axis=1)

    for c in (m_up, m_dn, m_sib, m_fwd, p_up, p_dn, p_up2, p_dn2, p_sib,
              p_fwd_a, p_fwd_b, p_fwd_c):
        c.wait_send()


def slot_maps(cols, counts, first_row, cycle):
    tile_rows, slot_count = cols.shape
    local = jnp.arange(tile_rows, dtype=jnp.int32)[:, None]
    place = (cols - (first_row + local) + BAND) % cycle + local
    live = jnp.arange(slot_count, dtype=jnp.int32)[None, :] < counts[:, None]
    width = tile_rows + 2 * BAND
    hit = (place[:, :, None] == jnp.arange(width, dtype=jnp.int32)) & live[:, :, None]
    slot = jnp.arange(slot_count, dtype=jnp.int32)[None, :, None]
    inverse = slot_count + jnp.sum(jnp.where(hit, slot - slot_count, 0), axis=1)
    return inverse, jnp.where(live, place, width)


def body(p_tiles, p_cols, p_count, m_tiles, m_cols, m_count, g_tiles, basis_atom, atom_slot):
    n = lax.axis_size("row")
    tile_rows = p_tiles.shape[0]
    cycle = tile_rows * n
    first_row = lax.axis_index("row") * tile_rows
    inv_p, idx_w = slot_maps(p_cols, p_count, first_row, cycle)
    inv_m, _ = slot_maps(m_cols, m_count, first_row, cycle)
    order = basis_atom.shape[0]
    span = (tile_rows + 2 * BAND) * 64
    wrapped = jnp.concatenate([basis_atom, basis_atom[:span]])
    start = (first_row * 64 - BAND * 64) % order
    atoms = lax.dynamic_slice_in_dim(wrapped, start, span)
    count = atom_slot.shape[0]
    cid = jnp.sum(jnp.where(atoms[:, None] == jnp.arange(count, dtype=jnp.int32)[None, :],
                            atom_slot[None, :], 0), axis=1, keepdims=True)
    smem = pl.BlockSpec(memory_space=pltpu.SMEM)
    vmem = pl.BlockSpec(memory_space=pltpu.VMEM)
    w, f = pl.pallas_call(
        functools.partial(kernel, n),
        out_shape=(jax.ShapeDtypeStruct((tile_rows, 64, 1024), F32),
                   jax.ShapeDtypeStruct((8, count), F32)),
        in_specs=[smem] * 3 + [vmem] * 4,
        out_specs=(vmem, vmem),
        scratch_shapes=[
            pltpu.VMEM((17, 256, 64), BF),
            pltpu.VMEM((17, 256, 64), BF),
            pltpu.VMEM((17, 256, 64), BF),
            pltpu.VMEM((256, 10 * L), BF),
            pltpu.VMEM((3, 256, 10 * L), BF),
            pltpu.VMEM((12 * L, 9 * L), BF),
            pltpu.VMEM((20 * L, 9 * L), BF),
            pltpu.VMEM((256, 18 * L), F32),
            pltpu.VMEM((256, 18 * L), BF),
            pltpu.VMEM((256, 10 * L), F32),
            pltpu.VMEM((21, 256, 64), F32),
            pltpu.VMEM((10 * L, count), BF),
            pltpu.SemaphoreType.DMA((4,)),
            pltpu.SemaphoreType.DMA((4,)),
            pltpu.SemaphoreType.DMA((8,)),
            pltpu.SemaphoreType.DMA((8,)),
        ],
        compiler_params=pltpu.CompilerParams(
            collective_id=0, has_side_effects=True, vmem_limit_bytes=56 * 1024 * 1024),
    )(inv_p, inv_m, idx_w, p_tiles, m_tiles, g_tiles, cid)
    forces = lax.psum_scatter(f[:3], "row", scatter_dimension=1, tiled=True)
    return w, forces


def solution(mesh):
    both = ("groups", "row")
    return jax.shard_map(
        body,
        mesh=mesh,
        in_specs=(P(both, None, None), P(both, None), P(both), P(both, None, None),
                  P(both, None), P(both), P(both, None, None, None), P("groups"), P("groups")),
        out_specs=(P(both, None, None), P(None, both)),
        check_vma=False,
    )
```

time: 509 us -> 135 us (0.27)
  local copies, waits for them, and re-layouts: 211 us -> 6.05 us
  waiting for transfers between devices: 102 us -> 0 us
  matrix products: 74.7 us -> 0 us
  Pallas kernels: 0 us -> 60.9 us
  blocking collectives: 0 us -> 60.4 us
  starting transfers between devices: 50.7 us -> 0 us
  other arithmetic: 44.7 us -> 5.61 us
  between operations: 14.4 us -> 1.33 us
  loops' own time: 10.3 us -> 0 us
    gather x16 -> x0, local copies, waits for them, and re-layouts: 129 us -> none  [the longest x4 42.7 us: one_row(): lax.dynamic_slice(m_band, (row_at, 0, start, 0), (1, tile_size, 4 * BAND...]
    dot_general x12 -> x0, matrix products: 74.7 us -> none  [the longest x4 20.5 us: one_row(): jnp.einsum('asb,sboc->aoc', own_grid[local], m_pieces, preferred_element_...]
    pallas_call x0 -> x1, Pallas kernels: none -> 60.9 us  [body(): pl.pallas_call(functools.partial(kernel, n), out_shape=(jax.ShapeDtypeStr...]
    unnamed x0 -> x1, blocking collectives: none -> 60.4 us
    unnamed x2 -> x0, waiting for transfers between devices: 51.4 us -> none
    ppermute x36 -> x0, starting transfers between devices: 50.7 us -> none  [passed_along(): lax.ppermute(array, axis, [(i, (i + by) % length) for i in range(length)])]
    ppermute x36 -> x0, waiting for transfers between devices: 50.1 us -> none  [passed_along(): lax.ppermute(array, axis, [(i, (i + by) % length) for i in range(length)])]
    reshape x6 -> x0, local copies, waits for them, and re-layouts: 30.6 us -> none  [the longest x2 18 us: band_form(): tile_grid = tiles.reshape(tile_rows, tile_size, slot_count, tile_size)]
  transfers between devices with their start and end apart: 37 -> 0, of which waited for: 17 -> 0; matrix products, arithmetic and copies ran while one was open for 21% -> 0% of each run, Pallas kernels for 0% -> 0%
where the time goes in v1:
time: 135 us; the launch traced here: 134 us
  Pallas kernels  60.9 us (45%)
  blocking collectives  60.4 us (45%)
  local copies, waits for them, and re-layouts  6.05 us (4%)
  other arithmetic  5.61 us (4%)
    pallas_call x1, Pallas kernels, body(): pl.pallas_call(functools.partial(kernel, n), out_shape=(jax.ShapeDtypeStr...  60.9 us
    unnamed x1, blocking collectives  60.4 us
    unnamed x5, local copies, waits for them, and re-layouts  3.55 us

profile of v1, /device:TPU:0, one launch (start us, length us, event | category | flops | bytes accessed | tf_op | source)
XLA Modules:
  0.0 134.2 jit_solution(4198669480594759953)
XLA Ops:
  0.7 0.7 slice.6
  1.4 0.8 fusion.2
  2.1 1.3 select_reduce_fusion
  3.4 1.1 broadcast_in_dim.60.cid_ref
  4.5 1.4 %broadcast_select_fusion = (s32[4,16]{1,0:T(4,128)}, s32[4,16]{1,0:T(4,128)S(1)}, s32[4,16]{1,0:T(4,128)S(1)}) fusion(s32[4]{0:T(128)} %param.11, s32[4,16]{1,0:T(4,128)} %param.10, s32[4]{0:T(128)S(1)} %iota_add_fusion.1, s32[4,16]{1,0:T(4,128)} %param.13), kind=kLoop, calls=%fused_computation.23 | loop fusion | flops 1920 | bytes 1312 | tf_op jit(solution)/shard_map/jit(_where)/select_n | solution.py:198
  5.9 0.7 iota_compare_fusion.3
  6.6 0.7 iota_compare_fusion.4
  7.3 0.1 select_reduce_fusion.1
  7.5 0.6 broadcast_add_fusion
  8.0 0.0 copy-start
  8.0 60.9 %shard_map.104 = (f32[4,64,1024]{2,1,0:T(8,128)}, f32[8,640]{1,0:T(8,128)}) custom-call(s32[4,20]{1,0:T(4,128)} %get-tuple-element.12.inv_p, s32[4,20]{1,0:T(4,128)} %get-tuple-element.11.inv_m, s32[4,16]{1,0:T(4,128)} %get-tuple-element.8.idx_w, bf16[4,64,1024]{2,1,0:T(8,128)(2,1)} %p_ref.1, bf16[4,64,1024]{2,1,0:T(8,128)(2,1)} %m_ref.1, ...), custom_call_target="tpu_custom_call" | custom-call | tf_op jit(solution)/shard_map/pallas_call | solution.py:218
  69.0 0.7 slice.7
  69.7 60.4 %all-reduce = f32[3,640]{1,0:T(4,128)S(1)} all-reduce(f32[3,640]{1,0:T(4,128)S(1)} %slice.7), channel_id=2, replica_groups=mesh['groups'=2,'row'=16] {'row'}, use_global_device_ids=true, to_apply=%region_3.4.clone | all-reduce | flops 1920 | bytes 15360
  130.0 0.0 copy-done
  130.0 0.6 dynamic-slice
  131.3 0.7 constant_dynamic-slice_fusion
  131.9 2.3 %copy.17 = f32[4,64,1024]{2,1,0:T(8,128)} copy(f32[4,64,1024]{2,1,0:T(8,128)} %get-tuple-element.15) | data formatting | bytes 2097152
  (2 shorter events, 0.0 us)
Async XLA Ops:
  8.0 122.0 %copy-start = (u32[32]{0:T(128)S(1)}, u32[32]{0:T(128)}, u32[]{:S(2)}) copy-start(u32[32]{0:T(128)} %constant.64) | copy-start | bytes 388

commit v2 on v1

v2 whole, which is shorter than its diff:
```python
import functools
import jax
import jax.numpy as jnp
from jax import lax
from jax.experimental import pallas as pl
from jax.experimental.pallas import tpu as pltpu
from jax.sharding import PartitionSpec as P

BAND = 8
L = 128
F32 = jnp.float32
BF = jnp.bfloat16
MESH = pl.DeviceIdType.MESH


def kernel(n, inverse, cols_p, count_p, p_ref, m_ref, g_ref, basis_ref, slot_ref, w_ref, f_ref,
           pt, mt, gt, pfull, gfull, mbuf, pbuf, xacc, xb, wacc, wt, onehot, fsend, frecv,
           ms, mr, ps, pr, fs, fr):
    me = lax.axis_index("row")
    core = lax.rem(me, 2)
    sibling = me + 1 - 2 * core

    def at(shift):
        return lax.rem(me + shift + n, n)

    side = 1 - 2 * lax.rem(lax.div(me, 2), 2)
    partner, onward, up2, dn2 = at(2 * side), at(4 * side), at(4), at(-4)
    barrier = pltpu.get_barrier_semaphore()

    def greet(i, carry):
        pl.semaphore_signal(barrier, inc=1, device_id={"row": at(i)}, device_id_type=MESH)
        return carry

    lax.fori_loop(1, n, greet, 0)

    def rows(at_super, count=2):
        return pl.ds(pl.multiple_of(at_super * L, L), count * L)

    def split(src, r, dst):
        for p in range(8):
            v = src[:, p * L:(p + 1) * L]
            dst[2 * p, r * 64:(r + 1) * 64, :] = v[:, :64]
            dst[2 * p + 1, r * 64:(r + 1) * 64, :] = v[:, 64:]
        dst[16, r * 64:(r + 1) * 64, :] = jnp.zeros((64, 64), BF)

    def pick(src, first, r, u):
        a = src[inverse[first + r, 2 * u], r * 64:(r + 1) * 64, :]
        b = src[inverse[first + r, 2 * u + 1], r * 64:(r + 1) * 64, :]
        return jnp.concatenate([a, b], axis=1)

    for r in range(4):
        split(m_ref.at[r], r, mt)
        sup = r // 2
        for u in range(sup, sup + 9):
            mbuf[pl.ds(pl.multiple_of((4 + 2 * core) * L, L) + r * 64, 64),
                 (u - sup) * L:(u - sup + 1) * L] = pick(mt, 4, r, u)
    pl.semaphore_wait(barrier, n - 1)

    def copy(buf, src_at, dst_at, col, width, sends, recvs, i, peer, count=2):
        cols = pl.ds(col, width * L)
        return pltpu.make_async_remote_copy(
            src_ref=buf.at[rows(src_at, count), cols], dst_ref=buf.at[rows(dst_at, count), cols],
            send_sem=sends.at[i], recv_sem=recvs.at[i],
            device_id={"row": peer}, device_id_type=MESH)

    own_m = 4 + 2 * core
    m_near, m_back = 4 + 4 * side + 2 * core, 4 - 4 * side + 2 * core
    m_par = [copy(mbuf, own_m + h, m_back + h, 0, 9, ms, mr, h, partner, 1) for h in range(2)]
    m_rel = [copy(mbuf, m_near + h, m_back + h, 0, 9, ms, mr, 2 + h, onward, 1) for h in range(2)]
    m_sib = copy(mbuf, own_m, own_m, 0, 9, ms, mr, 4, sibling)
    f_at = 8 - 6 * core
    m_fwd = copy(mbuf, f_at, f_at, 0, 9, ms, mr, 5, sibling)
    fwd_early = side == 1 - 2 * core
    m_par[0].start()
    m_par[1].start()
    m_sib.start()

    own_p = 8 + 2 * core
    for r in range(4):
        split(p_ref.at[r], r, pt)
        sup = r // 2
        for u in range(10):
            if sup <= u < sup + 9:
                v = pick(pt, 0, r, u)
                pfull[r * 64:(r + 1) * 64, u * L:(u + 1) * L] = v
                pbuf[pl.ds(pl.multiple_of(own_p * L, L) + r * 64, 64),
                     (u - sup) * L:(u - sup + 1) * L] = v
            else:
                pfull[r * 64:(r + 1) * 64, u * L:(u + 1) * L] = jnp.zeros((64, L), BF)
    p_near, p_back = 8 + 4 * side + 2 * core, 8 - 4 * side + 2 * core
    near_col = pl.multiple_of((1 - side) // 2 * L, L)
    back_col = pl.multiple_of((1 + side) // 2 * L, L)
    p_par = [copy(pbuf, own_p + h, p_back + h, 0, 9, ps, pr, h, partner, 1) for h in range(2)]
    p_rel = [copy(pbuf, p_near + h, p_back + h, back_col, 8, ps, pr, 2 + h, onward, 1)
             for h in range(2)]
    p_up2 = copy(pbuf, own_p, 2 * core, 5 * L, 4, ps, pr, 4, up2)
    p_dn2 = copy(pbuf, own_p, 16 + 2 * core, 0, 4, ps, pr, 5, dn2)
    p_sib = copy(pbuf, own_p, own_p, 0, 9, ps, pr, 6, sibling)
    p_fwd_a = copy(pbuf, p_near, p_near, near_col, 8, ps, pr, 7, sibling)
    p_fwd_b = copy(pbuf, p_back, p_back, back_col, 8, ps, pr, 8, sibling)
    far_at = 16 - 14 * core
    p_fwd_c = copy(pbuf, far_at, far_at, pl.multiple_of(core * 5 * L, L), 4, ps, pr, 9, sibling)
    for c in (*p_par, p_up2, p_dn2, p_sib):
        c.start()

    for c in range(3):
        for r in range(4):
            split(g_ref.at[r, c], r, gt)
            for u in range(10):
                gfull[c, r * 64:(r + 1) * 64, u * L:(u + 1) * L] = pick(gt, 0, r, u)
    slots = onehot.shape[0]
    lines = [basis_ref[pl.ds(lax.rem(2 * me - 4 + k + 2 * n, 2 * n), 1), :] for k in range(10)]
    atoms = jnp.concatenate(lines, axis=1)
    high_slot = slot_ref[...] // 64
    pair = jnp.concatenate([high_slot, slot_ref[...] - 64 * high_slot], axis=0).astype(F32)
    pair = jnp.concatenate([pair, jnp.zeros((6, slots), F32)], axis=0).astype(BF)

    def mark(values):
        for s in range(slots // L):
            ids = lax.broadcasted_iota(jnp.int32, (L, 10 * L), 0) + s * L
            onehot[s * L:(s + 1) * L, :] = jnp.where(values == ids, 1.0, 0.0).astype(BF)

    mark(atoms)
    found = jnp.dot(pair, onehot[...], preferred_element_type=F32)
    mark((64.0 * found[0:1] + found[1:2]).astype(jnp.int32))

    xacc[...] = jnp.zeros(xacc.shape, F32)
    wacc[...] = jnp.zeros(wacc.shape, F32)

    def add_x(j):
        xacc[:, j * L:(j + 9) * L] += jnp.dot(
            pfull[:, j * L:(j + 1) * L], mbuf[rows(j + 2 * core, 1), :],
            preferred_element_type=F32)

    def add_w(k):
        q0, q1 = max(0, 8 - k), min(8, 17 - k)
        m0 = k + q0 - 8
        width = q1 - q0 + 1
        wacc[:, m0 * L:(m0 + width) * L] += jnp.dot(
            xb[:, k * L:(k + 1) * L],
            pbuf[rows(k + 2 * core, 1), q0 * L:(q1 + 1) * L],
            preferred_element_type=F32)

    for h in range(2):
        m_par[h].wait_recv()
        m_rel[h].start()

    @pl.when(fwd_early)
    def _():
        m_fwd.start()

    add_x(4)
    add_x(5)
    for h in range(2):
        p_par[h].wait_recv()
        p_rel[h].start()
    p_fwd_a.start()
    p_up2.wait_recv()
    p_dn2.wait_recv()
    p_fwd_c.start()
    m_rel[0].wait_recv()
    m_rel[1].wait_recv()

    @pl.when(jnp.logical_not(fwd_early))
    def _():
        m_fwd.start()

    for j in (0, 1, 8, 9):
        add_x(j)
    m_sib.wait_recv()
    m_fwd.wait_recv()
    for j in (2, 3, 6, 7):
        add_x(j)
    xb[...] = xacc[...].astype(BF)
    for k in (8, 9, 0, 1, 16, 17):
        add_w(k)
    p_fwd_c.wait_recv()
    p_rel[0].wait_recv()
    p_rel[1].wait_recv()
    p_fwd_b.start()
    for k in (4, 5, 12, 13):
        add_w(k)
    p_sib.wait_recv()
    p_fwd_a.wait_recv()
    p_fwd_b.wait_recv()
    for k in (6, 7, 10, 11, 2, 3, 14, 15):
        add_w(k)

    lane = lax.broadcasted_iota(jnp.int32, (4 * 64, L), 1)
    by_row = jnp.zeros((4 * 64, L), F32)
    sub = lax.broadcasted_iota(jnp.int32, (8, 10 * L), 0)
    by_col = jnp.zeros((8, 10 * L), F32)
    for c in range(3):
        prod = wacc[...] * gfull[c].astype(F32)
        by_row = jnp.where(lane == c, jnp.sum(prod, axis=1, keepdims=True), by_row)
        by_col = jnp.where(sub == c, jnp.sum(prod, axis=0, keepdims=True), by_col)
    net_rows = jnp.transpose(by_row)[:8]
    net = jnp.concatenate(
        [-by_col[:, :4 * L], net_rows - by_col[:, 4 * L:6 * L], -by_col[:, 6 * L:]], axis=1)
    high = net.astype(BF).astype(F32)
    rest = net - high
    mid = rest.astype(BF).astype(F32)
    low = rest - mid
    parts = jnp.concatenate([high, mid, low, jnp.zeros_like(low)], axis=0).astype(BF)
    summed = lax.dot_general(parts, onehot[...], (((1,), (1,)), ((), ())),
                             preferred_element_type=F32)
    terms = -2.0 * (summed[0:8] + summed[8:16] + summed[16:24])
    share = slots // n
    for d in range(n):
        fsend[d, :, 0:share] = terms[:, d * share:(d + 1) * share]

    def force_copy(i):
        to = at(i)
        return pltpu.make_async_remote_copy(
            src_ref=fsend.at[to], dst_ref=frecv.at[i], send_sem=fs.at[i], recv_sem=fr.at[i],
            device_id={"row": to}, device_id_type=MESH)

    def force_start(i, carry):
        force_copy(i).start()
        return carry

    def force_wait(i, total):
        force_copy(i).wait_recv()
        return total + frecv[i]

    def force_done(i, carry):
        force_copy(i).wait_send()
        return carry

    lax.fori_loop(1, n, force_start, 0)

    for t in range(20):
        wt[t] = wacc[:, t * 64:(t + 1) * 64]
    wt[20] = jnp.zeros((4 * 64, 64), F32)

    def place(r, s):
        off = cols_p[r, s] - (4 * me + r) + BAND
        off = jnp.where(off < 0, off + 4 * n, off)
        off = jnp.where(off >= 4 * n, off - 4 * n, off)
        return jnp.where(s < count_p[r], off + r, 20)

    for r in range(4):
        for p in range(8):
            a = wt[place(r, 2 * p), r * 64:(r + 1) * 64, :]
            b = wt[place(r, 2 * p + 1), r * 64:(r + 1) * 64, :]
            w_ref[r, :, p * L:(p + 1) * L] = jnp.concatenate([a, b], axis=1)

    total = lax.fori_loop(1, n, force_wait, fsend[me])
    f_ref[...] = total[0:3, 0:share]
    lax.fori_loop(1, n, force_done, 0)
    for c in (*m_par, *m_rel, m_sib, m_fwd, *p_par, *p_rel, p_up2, p_dn2, p_sib,
              p_fwd_a, p_fwd_b, p_fwd_c):
        c.wait_send()


def slot_maps(cols, counts, first_row, cycle):
    lists, slot_count = cols.shape
    tile_rows = lists // 2
    local = (jnp.arange(lists, dtype=jnp.int32) % tile_rows)[:, None]
    place = (cols - (first_row + local) + BAND) % cycle + local
    slot = jnp.arange(slot_count, dtype=jnp.int32)[None, :]
    place = jnp.where(slot < counts[:, None], place, -1)
    hit = place[:, :, None] == jnp.arange(tile_rows + 2 * BAND, dtype=jnp.int32)
    return slot_count + jnp.sum(jnp.where(hit, slot[:, :, None] - slot_count, 0), axis=1)


def body(p_tiles, p_cols, p_count, m_tiles, m_cols, m_count, g_tiles, basis_atom, atom_slot):
    n = lax.axis_size("row")
    tile_rows = p_tiles.shape[0]
    first_row = lax.axis_index("row") * tile_rows
    inverse = slot_maps(jnp.concatenate([p_cols, m_cols]), jnp.concatenate([p_count, m_count]),
                        first_row, tile_rows * n)
    count = atom_slot.shape[0]
    smem = pl.BlockSpec(memory_space=pltpu.SMEM)
    vmem = pl.BlockSpec(memory_space=pltpu.VMEM)
    w, f = pl.pallas_call(
        functools.partial(kernel, n),
        out_shape=(jax.ShapeDtypeStruct((tile_rows, 64, 1024), F32),
                   jax.ShapeDtypeStruct((3, count // n), F32)),
        in_specs=[smem] * 3 + [vmem] * 5,
        out_specs=(vmem, vmem),
        scratch_shapes=[
            pltpu.VMEM((17, 256, 64), BF),
            pltpu.VMEM((17, 256, 64), BF),
            pltpu.VMEM((17, 256, 64), BF),
            pltpu.VMEM((256, 10 * L), BF),
            pltpu.VMEM((3, 256, 10 * L), BF),
            pltpu.VMEM((12 * L, 9 * L), BF),
            pltpu.VMEM((20 * L, 9 * L), BF),
            pltpu.VMEM((256, 18 * L), F32),
            pltpu.VMEM((256, 18 * L), BF),
            pltpu.VMEM((256, 10 * L), F32),
            pltpu.VMEM((21, 256, 64), F32),
            pltpu.VMEM((count, 10 * L), BF),
            pltpu.VMEM((n, 8, L), F32),
            pltpu.VMEM((n, 8, L), F32),
            pltpu.SemaphoreType.DMA((6,)),
            pltpu.SemaphoreType.DMA((6,)),
            pltpu.SemaphoreType.DMA((10,)),
            pltpu.SemaphoreType.DMA((10,)),
            pltpu.SemaphoreType.DMA((n,)),
            pltpu.SemaphoreType.DMA((n,)),
        ],
        compiler_params=pltpu.CompilerParams(
            collective_id=0, has_side_effects=True, vmem_limit_bytes=56 * 1024 * 1024),
    )(inverse, p_cols, p_count, p_tiles, m_tiles, g_tiles,
      basis_atom.reshape(-1, L), atom_slot.reshape(1, -1))
    return w, f


def solution(mesh):
    both = ("groups", "row")
    return jax.shard_map(
        body,
        mesh=mesh,
        in_specs=(P(both, None, None), P(both, None), P(both), P(both, None, None),
                  P(both, None), P(both), P(both, None, None, None), P("groups"), P("groups")),
        out_specs=(P(both, None, None), P(None, both)),
        check_vma=False,
    )
```

time: 135 us -> 62.5 us (0.46)
  blocking collectives: 60.4 us -> 0 us
  Pallas kernels: 60.9 us -> 55.1 us
  other arithmetic: 5.61 us -> 2.23 us
  local copies, waits for them, and re-layouts: 6.05 us -> 4.17 us
    unnamed x1 -> x0, blocking collectives: 60.4 us -> none
    pallas_call x1, Pallas kernels: 60.9 us -> 55.1 us  [body(): pl.pallas_call(functools.partial(kernel, n), out_shape=(jax.ShapeDtypeStr...]
    lt x2 -> x0, other arithmetic: 1.45 us -> none  [slot_maps(): live = jnp.arange(slot_count, dtype=jnp.int32)[None, :] < counts[:, None]]
    slice x2 -> x0, local copies, waits for them, and re-layouts: 1.43 us -> none  [the longest x1 0.73 us: body(): forces = lax.psum_scatter(f[:3], 'row', scatter_dimension=1, tiled=True)]
    unnamed x5 -> x4, local copies, waits for them, and re-layouts: 3.55 us -> 2.89 us
where the time goes in v2:
time: 62.5 us; the launch traced here: 62.2 us
  Pallas kernels  55.1 us (88%)
  local copies, waits for them, and re-layouts  4.17 us (7%)
  other arithmetic  2.23 us (4%)
  between operations  0.67 us (1%)
    pallas_call x1, Pallas kernels, body(): pl.pallas_call(functools.partial(kernel, n), out_shape=(jax.ShapeDtypeStr...  55.1 us
    unnamed x4, local copies, waits for them, and re-layouts  2.89 us
    reshape x1, local copies, waits for them, and re-layouts, body(): atom_slot.reshape(1, -1)  1.28 us

profile of v2, /device:TPU:0, one launch (start us, length us, event | category | flops | bytes accessed | tf_op | source)
XLA Modules:
  0.0 62.2 jit_solution(6364505466026913986)
XLA Ops:
  0.7 0.7 %and_select_fusion = (s32[8]{0:T(128)S(1)}, s32[8]{0:T(128)S(1)}) fusion(s32[4]{0:T(128)} %param.14, s32[4]{0:T(128)} %count_p.1), kind=kLoop, calls=%fused_computation.12 | loop fusion | flops 56 | bytes 96 | tf_op jit(solution)/shard_map/jit(remainder)/select_n | solution.py:259
  1.4 0.8 %fusion.2 = s32[8,16]{1,0:T(8,128)S(1)} fusion(s32[4,16]{1,0:T(4,128)} %param.13, s32[4,16]{1,0:T(4,128)} %cols_p.1, s32[8]{0:T(128)S(1)} %get-tuple-element.2, s32[8]{0:T(128)S(1)} %broadcast_add_fusion.1, s32[8]{0:T(128)S(1)} %get-tuple-element.3), kind=kLoop, calls=%fused_computation.7 | loop fusion | flops 2176 | bytes 1120 | tf_op jit(solution)/shard_map/jit(_where)/select_n | solution.py:262
  2.2 0.1 select_reduce_fusion
  2.3 0.6 broadcast_add_fusion.inverse
  2.9 1.3 %reshape.107.slot_ref = s32[1,640]{1,0:T(1,128)} reshape(s32[640]{0:T(1024)} %param.17) | data formatting | bytes 5120 | tf_op jit(solution)/shard_map/reshape | solution.py:307
  4.2 55.1 %shard_map.104 = (f32[4,64,1024]{2,1,0:T(8,128)}, f32[3,40]{1,0:T(4,128)}) custom-call(s32[8,20]{1,0:T(8,128)} %broadcast_add_fusion.inverse, s32[4,16]{1,0:T(4,128)} %cols_p.1, s32[4]{0:T(128)} %count_p.1, bf16[4,64,1024]{2,1,0:T(8,128)(2,1)} %p_ref.1, bf16[4,64,1024]{2,1,0:T(8,128)(2,1)} %m_ref.1, bf16[4,3,64,1024]{3,2,1,0:T(8,128)(2,1)} %g_ref.1, ...), custom_call_target="tpu_custom_call" | custom-call | tf_op jit(solution)/shard_map/pallas_call | solution.py:276
  59.3 0.0 copy-start
  59.3 2.3 %copy.13 = f32[4,64,1024]{2,1,0:T(8,128)} copy(f32[4,64,1024]{2,1,0:T(8,128)} %get-tuple-element.6) | data formatting | bytes 2097152
  61.6 0.0 copy-done
  61.6 0.6 copy.14
  (2 shorter events, 0.0 us)
Async XLA Ops:
  59.3 2.3 %copy-start = (f32[3,40]{1,0:T(4,128)S(1)}, f32[3,40]{1,0:T(4,128)}, u32[]{:S(2)}) copy-start(f32[3,40]{1,0:T(4,128)} %get-tuple-element.7) | copy-start | bytes 1444

commit v3 on v2

--- a/solution.py
+++ b/solution.py
@@ -91,17 +91,74 @@
     near_col = pl.multiple_of((1 - side) // 2 * L, L)
     back_col = pl.multiple_of((1 + side) // 2 * L, L)
     p_par = [copy(pbuf, own_p + h, p_back + h, 0, 9, ps, pr, h, partner, 1) for h in range(2)]
-    p_rel = [copy(pbuf, p_near + h, p_back + h, back_col, 8, ps, pr, 2 + h, onward, 1)
-             for h in range(2)]
-    p_up2 = copy(pbuf, own_p, 2 * core, 5 * L, 4, ps, pr, 4, up2)
-    p_dn2 = copy(pbuf, own_p, 16 + 2 * core, 0, 4, ps, pr, 5, dn2)
+    def in_case(act):
+        for way in (1, -1):
+            for b in range(2):
+                @pl.when(jnp.logical_and(side == way, core == b))
+                def _(way=way, b=b):
+                    act(way, b)
+
+    def back_cols(way, b, h):
+        return (4 - 2 * b - h, 5 + 2 * b + h) if way == 1 else (0, 8 - 2 * b - h)
+
+    def p_rel(way, b, h):
+        col, width = back_cols(way, b, h)
+        return copy(pbuf, p_near + h, p_back + h, col * L, width, ps, pr, 2 + h, onward, 1)
+
+    def p_fwd_b(way, b, h):
+        col, width = back_cols(way, b, h)
+        return copy(pbuf, p_back + h, p_back + h, col * L, width, ps, pr, 8 + h, sibling, 1)
+
+    def from_sib(way, b, h):
+        col, width = back_cols(way, 1 - b, h)
+        return copy(pbuf, p_back + h, p_back + h, col * L, width, ps, pr, 8 + h, sibling, 1)
+
+    def p_up2(b):
+        return copy(pbuf, own_p, 2 * core, (7 - 2 * b) * L, 2 + 2 * b, ps, pr, 4, up2)
+
+    def p_dn2(b):
+        return copy(pbuf, own_p, 16 + 2 * core, 0, 4 - 2 * b, ps, pr, 5, dn2)
+
     p_sib = copy(pbuf, own_p, own_p, 0, 9, ps, pr, 6, sibling)
     p_fwd_a = copy(pbuf, p_near, p_near, near_col, 8, ps, pr, 7, sibling)
-    p_fwd_b = copy(pbuf, p_back, p_back, back_col, 8, ps, pr, 8, sibling)
     far_at = 16 - 14 * core
-    p_fwd_c = copy(pbuf, far_at, far_at, pl.multiple_of(core * 5 * L, L), 4, ps, pr, 9, sibling)
-    for c in (*p_par, p_up2, p_dn2, p_sib):
-        c.start()
+    p_fwd_c = copy(pbuf, far_at, far_at, pl.multiple_of(core * 5 * L, L), 4, ps, pr, 10, sibling)
+    def start_far(way, b):
+        p_up2(b).start()
+        p_dn2(b).start()
+
+    p_par[0].start()
+    p_par[1].start()
+    in_case(start_far)
+    p_sib.start()
+
+    xacc[...] = jnp.zeros(xacc.shape, F32)
+    wacc[...] = jnp.zeros(wacc.shape, F32)
+
+    def add_x(j):
+        xacc[:, j * L:(j + 9) * L] += jnp.dot(
+            pfull[:, j * L:(j + 1) * L], mbuf[rows(j + 2 * core, 1), :],
+            preferred_element_type=F32)
+
+    def add_w(k):
+        q0, q1 = max(0, 8 - k), min(8, 17 - k)
+        m0 = k + q0 - 8
+        width = q1 - q0 + 1
+        wacc[:, m0 * L:(m0 + width) * L] += jnp.dot(
+            xb[:, k * L:(k + 1) * L],
+            pbuf[rows(k + 2 * core, 1), q0 * L:(q1 + 1) * L],
+            preferred_element_type=F32)
+
+    for h in range(2):
+        m_par[h].wait_recv()
+        m_rel[h].start()
+
+    @pl.when(fwd_early)
+    def _():
+        m_fwd.start()
+
+    add_x(4)
+    add_x(5)
 
     for c in range(3):
         for r in range(4):
@@ -111,8 +168,9 @@
     slots = onehot.shape[0]
     lines = [basis_ref[pl.ds(lax.rem(2 * me - 4 + k + 2 * n, 2 * n), 1), :] for k in range(10)]
     atoms = jnp.concatenate(lines, axis=1)
-    high_slot = slot_ref[...] // 64
-    pair = jnp.concatenate([high_slot, slot_ref[...] - 64 * high_slot], axis=0).astype(F32)
+    slot_row = jnp.concatenate([slot_ref[k:k + 1, :] for k in range(slots // L)], axis=1)
+    high_slot = slot_row // 64
+    pair = jnp.concatenate([high_slot, slot_row - 64 * high_slot], axis=0).astype(F32)
     pair = jnp.concatenate([pair, jnp.zeros((6, slots), F32)], axis=0).astype(BF)
 
     def mark(values):
@@ -124,39 +182,16 @@
     found = jnp.dot(pair, onehot[...], preferred_element_type=F32)
     mark((64.0 * found[0:1] + found[1:2]).astype(jnp.int32))
 
-    xacc[...] = jnp.zeros(xacc.shape, F32)
-    wacc[...] = jnp.zeros(wacc.shape, F32)
-
-    def add_x(j):
-        xacc[:, j * L:(j + 9) * L] += jnp.dot(
-            pfull[:, j * L:(j + 1) * L], mbuf[rows(j + 2 * core, 1), :],
-            preferred_element_type=F32)
-
-    def add_w(k):
-        q0, q1 = max(0, 8 - k), min(8, 17 - k)
-        m0 = k + q0 - 8
-        width = q1 - q0 + 1
-        wacc[:, m0 * L:(m0 + width) * L] += jnp.dot(
-            xb[:, k * L:(k + 1) * L],
-            pbuf[rows(k + 2 * core, 1), q0 * L:(q1 + 1) * L],
-            preferred_element_type=F32)
-
-    for h in range(2):
-        m_par[h].wait_recv()
-        m_rel[h].start()
-
-    @pl.when(fwd_early)
-    def _():
-        m_fwd.start()
-
-    add_x(4)
-    add_x(5)
     for h in range(2):
         p_par[h].wait_recv()
-        p_rel[h].start()
+        in_case(lambda way, b, h=h: p_rel(way, b, h).start())
     p_fwd_a.start()
-    p_up2.wait_recv()
-    p_dn2.wait_recv()
+
+    def wait_far(way, b):
+        p_up2(b).wait_recv()
+        p_dn2(b).wait_recv()
+
+    in_case(wait_far)
     p_fwd_c.start()
     m_rel[0].wait_recv()
     m_rel[1].wait_recv()
@@ -172,19 +207,34 @@
     for j in (2, 3, 6, 7):
         add_x(j)
     xb[...] = xacc[...].astype(BF)
-    for k in (8, 9, 0, 1, 16, 17):
-        add_w(k)
     p_fwd_c.wait_recv()
-    p_rel[0].wait_recv()
-    p_rel[1].wait_recv()
-    p_fwd_b.start()
-    for k in (4, 5, 12, 13):
-        add_w(k)
     p_sib.wait_recv()
     p_fwd_a.wait_recv()
-    p_fwd_b.wait_recv()
-    for k in (6, 7, 10, 11, 2, 3, 14, 15):
-        add_w(k)
+
+    def back_rows(way, b):
+        first = 8 - 4 * way
+        other = first + 2 - 4 * b
+        return (first, first + 1), (other, other + 1)
+
+    def early(way, b):
+        direct, handed = back_rows(way, b)
+        for k in range(18):
+            if k not in direct + handed:
+                add_w(k)
+
+    def late(way, b):
+        direct, handed = back_rows(way, b)
+        for h in range(2):
+            p_rel(way, b, h).wait_recv()
+            p_fwd_b(way, b, h).start()
+        for k in direct:
+            add_w(k)
+        for h in range(2):
+            from_sib(way, b, h).wait_recv()
+            add_w(handed[h])
+
+    in_case(early)
+    in_case(late)
 
     lane = lax.broadcasted_iota(jnp.int32, (4 * 64, L), 1)
     by_row = jnp.zeros((4 * 64, L), F32)
@@ -248,9 +298,17 @@
     total = lax.fori_loop(1, n, force_wait, fsend[me])
     f_ref[...] = total[0:3, 0:share]
     lax.fori_loop(1, n, force_done, 0)
-    for c in (*m_par, *m_rel, m_sib, m_fwd, *p_par, *p_rel, p_up2, p_dn2, p_sib,
-              p_fwd_a, p_fwd_b, p_fwd_c):
+    for c in (*m_par, *m_rel, m_sib, m_fwd, *p_par, p_sib, p_fwd_a, p_fwd_c):
         c.wait_send()
+
+    def sent(way, b):
+        p_up2(b).wait_send()
+        p_dn2(b).wait_send()
+        for h in range(2):
+            p_rel(way, b, h).wait_send()
+            p_fwd_b(way, b, h).wait_send()
+
+    in_case(sent)
 
 
 def slot_maps(cols, counts, first_row, cycle):
@@ -296,15 +354,15 @@
             pltpu.VMEM((n, 8, L), F32),
             pltpu.SemaphoreType.DMA((6,)),
             pltpu.SemaphoreType.DMA((6,)),
-            pltpu.SemaphoreType.DMA((10,)),
-            pltpu.SemaphoreType.DMA((10,)),
+            pltpu.SemaphoreType.DMA((11,)),
+            pltpu.SemaphoreType.DMA((11,)),
             pltpu.SemaphoreType.DMA((n,)),
             pltpu.SemaphoreType.DMA((n,)),
         ],
         compiler_params=pltpu.CompilerParams(
             collective_id=0, has_side_effects=True, vmem_limit_bytes=56 * 1024 * 1024),
     )(inverse, p_cols, p_count, p_tiles, m_tiles, g_tiles,
-      basis_atom.reshape(-1, L), atom_slot.reshape(1, -1))
+      basis_atom.reshape(-1, L), atom_slot.reshape(-1, L))
     return w, f
 
 

time: 62.5 us -> 55.6 us (0.89)
  Pallas kernels: 55.1 us -> 49.6 us
  local copies, waits for them, and re-layouts: 4.17 us -> 2.89 us
    pallas_call x1, Pallas kernels: 55.1 us -> 49.6 us  [body(): pl.pallas_call(functools.partial(kernel, n), out_shape=(jax.ShapeDtypeStr...]
    reshape x1 -> x0, local copies, waits for them, and re-layouts: 1.28 us -> none  [body(): atom_slot.reshape(1, -1)]
where the time goes in v3:
time: 55.6 us; the launch traced here: 55.4 us
  Pallas kernels  49.6 us (89%)
  local copies, waits for them, and re-layouts  2.89 us (5%)
  other arithmetic  2.23 us (4%)
  between operations  0.67 us (1%)
    pallas_call x1, Pallas kernels, body(): pl.pallas_call(functools.partial(kernel, n), out_shape=(jax.ShapeDtypeStr...  49.6 us
    unnamed x4, local copies, waits for them, and re-layouts  2.89 us

profile of v3, /device:TPU:0, one launch (start us, length us, event | category | flops | bytes accessed | tf_op | source)
XLA Modules:
  0.0 55.4 jit_solution(3640491589712415518)
XLA Ops:
  0.7 0.7 %and_select_fusion = (s32[8]{0:T(128)S(1)}, s32[8]{0:T(128)S(1)}) fusion(s32[4]{0:T(128)} %param.14, s32[4]{0:T(128)} %count_p.1), kind=kLoop, calls=%fused_computation.12 | loop fusion | flops 56 | bytes 96 | tf_op jit(solution)/shard_map/jit(remainder)/select_n | solution.py:317
  1.4 0.8 %fusion.2 = s32[8,16]{1,0:T(8,128)S(1)} fusion(s32[4,16]{1,0:T(4,128)} %param.13, s32[4,16]{1,0:T(4,128)} %cols_p.1, s32[8]{0:T(128)S(1)} %get-tuple-element.2, s32[8]{0:T(128)S(1)} %broadcast_add_fusion.1, s32[8]{0:T(128)S(1)} %get-tuple-element.3), kind=kLoop, calls=%fused_computation.7 | loop fusion | flops 2176 | bytes 1120 | tf_op jit(solution)/shard_map/jit(_where)/select_n | solution.py:320
  2.2 0.1 select_reduce_fusion
  2.3 0.6 %broadcast_add_fusion.inverse = s32[8,20]{1,0:T(8,128)} fusion(s32[8,20]{1,0:T(8,128)S(1)} %select_reduce_fusion), kind=kLoop, calls=%fused_computation.11 | loop fusion | flops 160 | bytes 1280 | tf_op jit(solution)/shard_map/add | solution.py:322
  2.9 49.6 %shard_map.104 = (f32[4,64,1024]{2,1,0:T(8,128)}, f32[3,40]{1,0:T(4,128)}) custom-call(s32[8,20]{1,0:T(8,128)} %broadcast_add_fusion.inverse, s32[4,16]{1,0:T(4,128)} %cols_p.1, s32[4]{0:T(128)} %count_p.1, bf16[4,64,1024]{2,1,0:T(8,128)(2,1)} %p_ref.1, bf16[4,64,1024]{2,1,0:T(8,128)(2,1)} %m_ref.1, bf16[4,3,64,1024]{3,2,1,0:T(8,128)(2,1)} %g_ref.1, ...), custom_call_target="tpu_custom_call" | custom-call | tf_op jit(solution)/shard_map/pallas_call | solution.py:334
  52.5 0.0 copy-start
  52.5 2.3 %copy.13 = f32[4,64,1024]{2,1,0:T(8,128)} copy(f32[4,64,1024]{2,1,0:T(8,128)} %get-tuple-element.6) | data formatting | bytes 2097152
  54.9 0.0 copy-done
  54.9 0.6 %copy.14 = f32[3,40]{1,0:T(4,128)} copy(f32[3,40]{1,0:T(4,128)S(1)} %copy-done) | data formatting | bytes 960
  (2 shorter events, 0.0 us)
Async XLA Ops:
  52.5 2.3 %copy-start = (f32[3,40]{1,0:T(4,128)S(1)}, f32[3,40]{1,0:T(4,128)}, u32[]{:S(2)}) copy-start(f32[3,40]{1,0:T(4,128)} %get-tuple-element.7) | copy-start | bytes 1444
